TPU v7x, 32 devices: a whole 2x2x4 slice. The times are simulated.
32 devices in a mesh: groups: 2 (over y), pfx: 4 (over z), smp: 2 (over x), kv: 2 (over core).
Axes of the slice: x: 2, y: 2, z: 4, core: 2. Of those that a mesh axis runs over, the one named last changes fastest.
Arguments:
- hidden: bfloat16 [64, 8192], P(('groups', 'smp'), 'pfx'), parts along dimension 0, may hold values from -6 to 6
- norm_gain: bfloat16 [8192], P('pfx'), may hold values from 0.5 to 1.5
- query_weight: bfloat16 [8192, 4096], P('pfx', 'kv'), may hold values from -0.0625 to 0.0625
- key_matrix: bfloat16 [8192, 512], P('pfx', 'kv'), may hold values from -0.52734375 to 0.52734375
- value_matrix: bfloat16 [8192, 512], P('pfx', 'kv'), may hold values from -0.0625 to 0.0625
- prefix_key: bfloat16 [16384, 512], P(('groups', 'pfx', 'smp'), 'kv'), parts along dimension 0, may hold values from -160 to 160
- shared_prefix_value: bfloat16 [16384, 512], P(('groups', 'pfx', 'smp'), 'kv'), parts along dimension 0, may hold values from -6 to 6
- sample_suffix_key: bfloat16 [64, 128, 512], P(('groups', 'smp'), 'pfx', 'kv'), parts along dimension 0, may hold values from -24 to 24
- sample_suffix_value: bfloat16 [64, 128, 512], P(('groups', 'smp'), 'pfx', 'kv'), parts along dimension 0, may hold values from -6 to 6
- lengths: int32 [64], P(('groups', 'smp')), parts along dimension 0, may hold values from 1 to 128, as said below
- assign: int32 [64], P(('groups', 'smp')), parts along dimension 0, may hold values from 0 to 31, as said below
Outputs:
- attended: bfloat16 [64, 4096], P(('groups', 'smp'), 'kv'), parts along dimension 0
There are 2 independent parts, one for each index of `groups`. A program takes and returns all parts, laid end to end along the dimension named above; an argument that names none is the same for every part. Nothing has to cross between parts.
Inputs may be any that keep to these rules, and one draw needn't show every extreme that they name: `lengths`: some sample has exactly 128 live positions. `assign`: each aligned block of 16 rows holds each sample number of that block once.
All inputs are finite; a program needn't handle non-finite values.
Results may differ from a plain program's by a relative error of at most 0.017.
Values may be sent and summed in bfloat16 or wider, within the bound.
A program may use at most 64 MiB of HBM per device.

v0:
```python
import jax
import jax.numpy as jnp
from jax import lax
from jax.sharding import PartitionSpec as P

MODEL_WIDTH = 8192
HEAD_WIDTH = 128


norm_eps = 1e-05
very_negative = -1e30


def prefix_head(operands):
    query_block, key_block, value_block = operands
    scores = jnp.einsum(
        "bgd,kd->bgk", query_block, key_block, preferred_element_type=jnp.float32
    ) * HEAD_WIDTH ** (-0.5)
    top_score = jnp.max(scores, axis=2)
    weights = jnp.exp(scores - top_score[..., None]).astype(jnp.bfloat16)
    denominator = jnp.sum(weights.astype(jnp.float32), axis=2)
    numerator = jnp.einsum("bgk,kd->bgd", weights, value_block, preferred_element_type=jnp.float32)
    return (numerator, denominator, top_score)


def body(
    hidden,
    norm_gain,
    query_weight,
    key_matrix,
    value_matrix,
    prefix_key,
    shared_prefix_value,
    sample_suffix_key,
    sample_suffix_value,
    lengths,
    assign,
):
    local_rows = hidden.shape[0]
    local_kv = key_matrix.shape[1] // HEAD_WIDTH
    local_heads = query_weight.shape[1] // HEAD_WIDTH
    group_width = local_heads // local_kv
    score_scale = HEAD_WIDTH ** (-0.5)
    hidden_wide = hidden.astype(jnp.float32)
    normed = (hidden_wide * norm_gain.astype(jnp.float32)).astype(jnp.bfloat16)
    query_part = jnp.dot(normed, query_weight, preferred_element_type=jnp.float32)
    key_part = jnp.dot(normed, key_matrix, preferred_element_type=jnp.float32)
    value_part = jnp.dot(normed, value_matrix, preferred_element_type=jnp.float32)
    square_part = jnp.sum(hidden_wide * hidden_wide, axis=1)
    query_sum, key_sum, value_sum, square_sum = lax.psum(
        (query_part, key_part, value_part, square_part), "pfx"
    )
    rms_value = jnp.sqrt(square_sum / MODEL_WIDTH + norm_eps)
    query_rows = (query_sum / rms_value[:, None]).astype(jnp.bfloat16)
    new_key = (key_sum / rms_value[:, None]).astype(jnp.bfloat16)
    new_value = (value_sum / rms_value[:, None]).astype(jnp.bfloat16)
    all_queries = lax.all_gather(query_rows, "smp", axis=0, tiled=True)
    sample_count = all_queries.shape[0]
    head_queries = jnp.transpose(
        all_queries.reshape(sample_count, local_kv, group_width, HEAD_WIDTH), (1, 0, 2, 3)
    )
    head_keys = jnp.transpose(prefix_key.reshape(-1, local_kv, HEAD_WIDTH), (1, 0, 2))
    head_values = jnp.transpose(shared_prefix_value.reshape(-1, local_kv, HEAD_WIDTH), (1, 0, 2))
    pre_numer, pre_denom, pre_top = lax.map(prefix_head, (head_queries, head_keys, head_values))
    pre_numer = jnp.transpose(pre_numer, (1, 0, 2, 3)).reshape(
        sample_count, local_heads, HEAD_WIDTH
    )
    pre_denom = jnp.transpose(pre_denom, (1, 0, 2)).reshape(sample_count, local_heads)
    pre_top = jnp.transpose(pre_top, (1, 0, 2)).reshape(sample_count, local_heads)
    row_base = lax.axis_index("smp") * local_rows
    slot_index = assign - row_base
    one_hot = (slot_index[:, None] == jnp.arange(local_rows, dtype=jnp.int32)[None, :]).astype(
        jnp.float32
    )
    slot_query = jnp.einsum(
        "rs,rx->sx", one_hot, query_rows.astype(jnp.float32), precision=lax.Precision.HIGHEST
    ).astype(jnp.bfloat16)
    slot_query = slot_query.reshape(local_rows, local_kv, group_width, HEAD_WIDTH)
    suffix_len = sample_suffix_key.shape[1]
    suffix_keys = sample_suffix_key.reshape(local_rows, suffix_len, local_kv, HEAD_WIDTH)
    suffix_values = sample_suffix_value.reshape(local_rows, suffix_len, local_kv, HEAD_WIDTH)
    suffix_scores = (
        jnp.einsum("shgd,sthd->shgt", slot_query, suffix_keys, preferred_element_type=jnp.float32)
        * score_scale
    )
    position = lax.axis_index("pfx") * suffix_len + jnp.arange(suffix_len, dtype=jnp.int32)
    live_mask = (position[None, :] < lengths[:, None])[:, None, None, :]
    suffix_scores = jnp.where(live_mask, suffix_scores, very_negative)
    suffix_top = jnp.max(suffix_scores, axis=3)
    suffix_weights = jnp.where(
        live_mask, jnp.exp(suffix_scores - suffix_top[..., None]), 0.0
    ).astype(jnp.bfloat16)
    suffix_denom = jnp.sum(suffix_weights.astype(jnp.float32), axis=3)
    suffix_numer = jnp.einsum(
        "shgt,sthd->shgd", suffix_weights, suffix_values, preferred_element_type=jnp.float32
    )
    row_numer = jnp.einsum(
        "rs,shgd->rhgd", one_hot, suffix_numer, precision=lax.Precision.HIGHEST
    ).reshape(local_rows, local_heads, HEAD_WIDTH)
    row_denom = jnp.einsum(
        "rs,shg->rhg", one_hot, suffix_denom, precision=lax.Precision.HIGHEST
    ).reshape(local_rows, local_heads)
    row_top = jnp.einsum(
        "rs,shg->rhg", one_hot, suffix_top, precision=lax.Precision.HIGHEST
    ).reshape(local_rows, local_heads)
    full_top = lax.dynamic_update_slice(
        jnp.full((sample_count, local_heads), very_negative, jnp.float32), row_top, (row_base, 0)
    )
    local_top = jnp.maximum(pre_top, full_top)
    global_top = lax.pmax(local_top, ("pfx", "smp"))
    own_top = lax.dynamic_slice_in_dim(global_top, row_base, local_rows, 0)
    pre_factor = jnp.exp(pre_top - global_top)
    row_factor = jnp.exp(row_top - own_top)
    scaled_row_numer = row_numer * row_factor[..., None]
    scaled_row_denom = row_denom * row_factor
    term_numer = pre_numer * pre_factor[..., None]
    term_denom = pre_denom * pre_factor
    term_numer = lax.dynamic_update_slice(
        term_numer,
        lax.dynamic_slice_in_dim(term_numer, row_base, local_rows, 0) + scaled_row_numer,
        (row_base, 0, 0),
    )
    term_denom = lax.dynamic_update_slice(
        term_denom,
        lax.dynamic_slice_in_dim(term_denom, row_base, local_rows, 0) + scaled_row_denom,
        (row_base, 0),
    )
    block_numer, block_denom = (
        lax.psum_scatter(
            term_numer.astype(jnp.bfloat16), "smp", scatter_dimension=0, tiled=True
        ).astype(jnp.float32),
        lax.psum_scatter(
            term_denom.astype(jnp.bfloat16), "smp", scatter_dimension=0, tiled=True
        ).astype(jnp.float32),
    )
    numerator, denominator = (
        lax.psum(block_numer.astype(jnp.bfloat16), "pfx").astype(jnp.float32),
        lax.psum(block_denom.astype(jnp.bfloat16), "pfx").astype(jnp.float32),
    )
    query_wide = query_rows.reshape(local_rows, local_kv, group_width, HEAD_WIDTH).astype(
        jnp.float32
    )
    own_key = new_key.reshape(local_rows, local_kv, 1, HEAD_WIDTH).astype(jnp.float32)
    own_score = (jnp.sum(query_wide * own_key, axis=3) * score_scale).reshape(
        local_rows, local_heads
    )
    final_top = jnp.maximum(own_top, own_score)
    old_factor = jnp.exp(own_top - final_top)
    own_weight = lax.optimization_barrier(
        jnp.exp(own_score - final_top).astype(jnp.bfloat16)
    ).astype(jnp.float32)
    own_value = jnp.broadcast_to(
        new_value.reshape(local_rows, local_kv, 1, HEAD_WIDTH).astype(jnp.float32),
        (local_rows, local_kv, group_width, HEAD_WIDTH),
    ).reshape(local_rows, local_heads, HEAD_WIDTH)
    numerator = numerator * old_factor[..., None] + own_weight[..., None] * own_value
    denominator = denominator * old_factor + own_weight
    return (
        (numerator / denominator[..., None])
        .astype(jnp.bfloat16)
        .reshape(local_rows, local_heads * HEAD_WIDTH)
    )


def solution(mesh):
    return jax.shard_map(
        body,
        mesh=mesh,
        in_specs=(
            P(("groups", "smp"), "pfx"),
            P("pfx"),
            P("pfx", "kv"),
            P("pfx", "kv"),
            P("pfx", "kv"),
            P(("groups", "pfx", "smp"), "kv"),
            P(("groups", "pfx", "smp"), "kv"),
            P(("groups", "smp"), "pfx", "kv"),
            P(("groups", "smp"), "pfx", "kv"),
            P(("groups", "smp")),
            P(("groups", "smp")),
        ),
        out_specs=P(("groups", "smp"), "kv"),
        check_vma=False,
    )
```

profile of v0, /device:TPU:0, one launch (start us, length us, event | category | flops | bytes accessed | tf_op | source)
XLA Modules:
  0.0 150.8 jit_solution(18185746916683848563)
XLA Ops:
  6.5 0.8 convert_element_type.89
  7.4 5.4 %fusion.30 = f32[16,2048]{1,0:T(8,128)} fusion(bf16[2048,2048]{1,0:T(8,128)(2,1)} %param.15, bf16[16,2048]{1,0:T(8,128)(2,1)} %param.13, f32[2048]{0:T(1024)S(1)} %convert_element_type.89), kind=kOutput, calls=%fused_computation.49 | convolution fusion | flops 134316032 | bytes 8593408 | tf_op jit(solution)/shard_map/dot_general | solution.py:46
  14.0 21.3 %all-reduce = (f32[16]{0:T(128)S(1)}, f32[16,256]{1,0:T(8,128)S(1)}, f32[16,256]{1,0:T(8,128)S(1)}) all-reduce(f32[16]{0:T(128)S(1)} %fusion.18, f32[16,256]{1,0:T(8,128)S(1)} %fusion.28, f32[16,256]{1,0:T(8,128)S(1)} %fusion.26), channel_id=1, replica_groups=mesh['groups'=2,'pfx'=4,'smp'=2,'kv'=2] {'pfx'}, use_global_device_ids=true, to_apply=%region_2.0 | all-reduce | flops 8208 | bytes 65664 | tf_op jit(solution)/shard_map/psum | solution.py:50
  35.9 0.7 broadcast_compare_fusion
  36.6 0.7 broadcast_subtract_fusion
  37.3 13.0 %all-reduce.4.cloned.1.call-done = f32[16,2048]{1,0:T(8,128)} async-done(((f32[16,2048]{1,0:T(8,128)}), f32[16,2048]{1,0:T(8,128)}) %all-reduce.4.cloned.1.call-update) | async-done | bytes 131088 | tf_op jit(solution)/shard_map/psum | solution.py:50
  50.2 1.0 convert_bitcast_fusion
  51.5 4.9 %all_gather.3 = bf16[32,2048]{1,0:T(8,128)(2,1)S(1)} all-gather(bf16[16,2048]{1,0:T(8,128)(2,1)S(1)} %get-tuple-element.97), channel_id=1, replica_groups=mesh['groups'=2,'pfx'=4,'smp'=2,'kv'=2] {'smp'}, dimensions={0}, use_global_device_ids=true | all-gather | bytes 196608 | tf_op jit(solution)/shard_map/all_gather | solution.py:57
  57.6 1.2 fusion.12
  59.1 4.6 %while.14 = (s32[]{:T(128)}, f32[2,32,8,128]{3,2,0,1:T(8,128)}, f32[2,32,8]{2,1,0:T(8,128)}, f32[2,32,8]{2,1,0:T(8,128)S(1)}, bf16[2,32,8,128]{3,2,1,0:T(8,128)(...) while((s32[]{:T(128)}, f32[2,32,8,128]{3,2,0,1:T(8,128)}, ...), condition=%wide.region_6.7_spmd, body=%wide.region_3.6_spmd.sunk | while | flops 136314368 | bytes 3953761 | solution.py:64
  59.8 1.0 fusion.64
  60.8 0.6 bitcast_dynamic-update-slice_fusion.3
  62.1 1.0 fusion.64
  64.0 20.4 %pmax.7 = f32[32,16]{0,1:T(8,128)S(1)} all-reduce(f32[32,16]{0,1:T(8,128)S(1)} %bitcast_maximum_fusion), channel_id=1, replica_groups=mesh['groups'=2,'pfx'=4,'smp'=2,'kv'=2] {'pfx','smp'}, use_global_device_ids=true, to_apply=%region_8.9 | all-reduce | flops 512 | bytes 4096 | tf_op jit(solution)/shard_map/pmax | solution.py:110
  84.6 0.8 copy.71
  85.8 0.7 copy.75
  86.6 1.1 bitcast_multiply_fusion
  87.8 0.7 convert_element_type.94
  88.7 5.0 %reduce-scatter.7.cloned.1.call-done = bf16[16,16]{1,0:T(8,128)(2,1)} async-done(((bf16[32,16]{1,0:T(8,128)(2,1)}), bf16[16,16]{1,0:T(8,128)(2,1)}) %reduce-scatter.7.cloned.1.call-update) | async-done | bytes 528
  93.7 0.7 copy.76
  94.4 11.7 %psum.47 = bf16[16,16]{0,1:T(8,128)(2,1)S(1)} all-reduce(bf16[16,16]{0,1:T(8,128)(2,1)S(1)} %copy.76), channel_id=1, replica_groups=mesh['groups'=2,'pfx'=4,'smp'=2,'kv'=2] {'pfx'}, use_global_device_ids=true, to_apply=%region_16.17 | all-reduce | flops 256 | bytes 1024 | tf_op jit(solution)/shard_map/psum | solution.py:138
  106.5 36.0 %all-reduce.6.cloned.1.call-done = bf16[16,16,128]{2,1,0:T(8,128)(2,1)} async-done(((bf16[16,16,128]{2,1,0:T(8,128)(2,1)}), bf16[16,16,128]{2,1,0:T(8,128)(2,1)}) %all-reduce.6.cloned.1.call-update) | async-done | bytes 65552 | tf_op jit(solution)/shard_map/psum | solution.py:137
  142.6 1.0 fusion.21
  143.6 0.6 copy.110
  (70 shorter events, 7.0 us)
Async XLA Ops:
  6.5 7.0 %copy-start = (bf16[2048,256]{1,0:T(8,128)(2,1)S(1)}, bf16[2048,256]{1,0:T(8,128)(2,1)}, u32[]{:S(2)}) copy-start(bf16[2048,256]{1,0:T(8,128)(2,1)} %param.16) | copy-start | bytes 3145732
  6.5 6.3 %copy-start.1 = (bf16[16,2048]{1,0:T(8,128)(2,1)S(1)}, bf16[16,2048]{1,0:T(8,128)(2,1)}, u32[]{:S(2)}) copy-start(bf16[16,2048]{1,0:T(8,128)(2,1)} %param.13) | copy-start | bytes 196612
  6.5 43.7 %all-reduce.4.cloned.1.call-start = ((), (), s32[]{:S(2)}) async-start(), calls=%async_computation.2 | async-start | bytes 262144 | tf_op jit(solution)/shard_map/psum | solution.py:50
  7.3 6.5 %copy-start.2 = (bf16[2048,256]{1,0:T(8,128)(2,1)S(1)}, bf16[2048,256]{1,0:T(8,128)(2,1)}, u32[]{:S(2)}) copy-start(bf16[2048,256]{1,0:T(8,128)(2,1)} %param.17) | copy-start | bytes 3145732
  7.3 28.2 %copy-start.3 = (bf16[1024,256]{1,0:T(8,128)(2,1)S(1)}, bf16[1024,256]{1,0:T(8,128)(2,1)}, u32[]{:S(2)}) copy-start(bf16[1024,256]{1,0:T(8,128)(2,1)} %param.18) | copy-start | bytes 1572868
  7.3 28.4 %copy-start.4 = (bf16[1024,256]{1,0:T(8,128)(2,1)S(1)}, bf16[1024,256]{1,0:T(8,128)(2,1)}, u32[]{:S(2)}) copy-start(bf16[1024,256]{1,0:T(8,128)(2,1)} %param.19) | copy-start | bytes 1572868
  7.3 28.6 %copy-start.6 = (s32[16]{0:T(128)S(1)}, s32[16]{0:T(128)}, u32[]{:S(2)}) copy-start(s32[16]{0:T(128)} %param.22) | copy-start | bytes 196
  7.3 49.4 %copy-start.5 = (bf16[16,32,256]{2,1,0:T(8,128)(2,1)S(1)}, bf16[16,32,256]{2,1,0:T(8,128)(2,1)}, u32[]{:S(2)}) copy-start(bf16[16,32,256]{2,1,0:T(8,128)(2,1)} %param.20) | copy-start | bytes 786436
  12.8 80.9 %reduce-scatter.7.cloned.1.call-start = ((), (), s32[]{:S(2)}) async-start(), calls=%async_computation.5 | async-start | bytes 12288
  86.5 19.8 %reduce-scatter.5.cloned.1.call-start = ((), (), s32[]{:S(2)}) async-start(), calls=%async_computation.3 | async-start | bytes 196608 | tf_op jit(solution)/shard_map/reduce_scatter | solution.py:129
  88.5 54.1 %all-reduce.6.cloned.1.call-start = ((), (), s32[]{:S(2)}) async-start(), calls=%async_computation.4 | async-start | bytes 131072 | tf_op jit(solution)/shard_map/psum | solution.py:137
Sparse Core Ops, SparseCore 0:
  12.9 37.2 all-reduce.3
  86.6 7.0 reduce-scatter.6
  96.0 10.2 reduce-scatter.4
  108.6 33.9 all-reduce.5
where the time goes:
time: 151 us
  blocking collectives  58.3 us (39%)
  waiting for transfers between devices  54.3 us (36%)
  between operations  13.4 us (9%)
  matrix products  11.2 us (7%)
  other arithmetic  7.82 us (5%)
  local copies, waits for them, and re-layouts  5.68 us (4%)
    psum x1, waiting for transfers between devices, body(): lax.psum(block_numer.astype(jnp.bfloat16), 'pfx').astype(jnp.float32)  36 us
    psum x1, blocking collectives, body(): lax.psum((query_part, key_part, value_part, square_part), 'pfx')  21.3 us
    pmax x1, blocking collectives, body(): global_top = lax.pmax(local_top, ('pfx', 'smp'))  20.4 us
    psum x1, waiting for transfers between devices, body(): lax.psum((query_part, key_part, value_part, square_part), 'pfx')  13 us
    psum x1, blocking collectives, body(): lax.psum(block_denom.astype(jnp.bfloat16), 'pfx').astype(jnp.float32)  11.7 us
    dot_general x1, matrix products, body(): jnp.dot(normed, query_weight, preferred_element_type=jnp.float32)  5.42 us
    unnamed x5, waiting for transfers between devices  5.1 us
    all_gather x1, blocking collectives, body(): all_queries = lax.all_gather(query_rows, 'smp', axis=0, tiled=True)  4.94 us
  transfers between devices with their start and end apart: 4, of which 4 were waited for; matrix products, arithmetic and copies ran while one was open for 4% of the time, Pallas kernels for 0%

commit v1 on v0

--- a/solution.py
+++ b/solution.py
@@ -1,6 +1,11 @@
+import functools
+import math
+
 import jax
 import jax.numpy as jnp
 from jax import lax
+from jax.experimental import pallas as pl
+from jax.experimental.pallas import tpu as pltpu
 from jax.sharding import PartitionSpec as P
 
 MODEL_WIDTH = 8192
@@ -23,7 +28,7 @@
     return (numerator, denominator, top_score)
 
 
-def body(
+def plain_body(
     hidden,
     norm_gain,
     query_weight,
@@ -162,9 +167,448 @@
     )
 
 
+def group_kernel(
+    pfx,
+    smp,
+    hidden_hbm,
+    gain_ref,
+    query_weight_hbm,
+    key_matrix_hbm,
+    value_matrix_hbm,
+    prefix_key_hbm,
+    prefix_value_hbm,
+    suffix_key_hbm,
+    suffix_value_hbm,
+    lengths_ref,
+    assign_ref,
+    out_ref,
+    hidden_v,
+    normed_v,
+    query_weight_v,
+    new_weight_v,
+    keys_v,
+    values_v,
+    flipped_v,
+    bias_v,
+    square_v,
+    query_part,
+    query_recv,
+    new_part,
+    new_recv,
+    queries_v,
+    numer_send,
+    stat_send,
+    numer_recv,
+    stat_recv,
+    column_v,
+    out_v,
+    load_sem,
+    square_sems,
+    query_sems,
+    new_sems,
+    gather_sems,
+    numer_sems,
+    stat_sems,
+    out_sems,
+):
+    rows, width = hidden_v.shape
+    kv_heads, key_count, _ = keys_v.shape
+    prefix_count = prefix_key_hbm.shape[0]
+    suffix_count = suffix_key_hbm.shape[0]
+    suffix_len = suffix_count // rows
+    piece_cols = query_weight_v.shape[2]
+    piece_heads = piece_cols // HEAD_WIDTH
+    piece_rows = piece_heads * rows
+    lanes = smp * piece_rows
+    pieces_per_kv = pfx // kv_heads
+    sources = pfx * smp
+    power_scale = HEAD_WIDTH ** (-0.5) * math.log2(math.e)
+
+    p = lax.axis_index("pfx")
+    s = lax.axis_index("smp")
+    me = p * smp + s
+
+    def other_p(step):
+        return lax.rem(p + step, pfx)
+
+    def other_s(step):
+        return lax.rem(s + step, smp)
+
+    steps = sorted(range(1, pfx), key=lambda step: -min(step, pfx - step))
+    order = steps + [0]
+    peers = [(a, b) for a in [0] + steps for b in range(smp) if (a, b) != (0, 0)]
+
+    def remote(source, target, sems, send_index, recv_index, to_p, to_s):
+        return pltpu.make_async_remote_copy(
+            src_ref=source,
+            dst_ref=target,
+            send_sem=sems.at[0, send_index],
+            recv_sem=sems.at[1, recv_index],
+            device_id={"pfx": to_p, "smp": to_s},
+            device_id_type=pl.DeviceIdType.MESH,
+        )
+
+    loads = []
+
+    def load(source, target):
+        copy = pltpu.make_async_copy(source, target, load_sem.at[len(loads)])
+        copy.start()
+        loads.append(copy)
+        return copy
+
+    hidden_load = load(hidden_hbm, hidden_v)
+    query_loads = []
+    for slot, step in enumerate(order):
+        start = pl.multiple_of(other_p(step) * piece_cols, piece_cols)
+        query_loads.append(
+            load(query_weight_hbm.at[:, pl.ds(start, piece_cols)], query_weight_v.at[slot])
+        )
+    new_loads = [
+        load(key_matrix_hbm, new_weight_v.at[0]),
+        load(value_matrix_hbm, new_weight_v.at[1]),
+    ]
+    value_loads, key_loads = [], []
+    for g in range(kv_heads):
+        head = pl.ds(g * HEAD_WIDTH, HEAD_WIDTH)
+        early, late = pl.ds(0, prefix_count), pl.ds(prefix_count, suffix_count)
+        value_loads.append(load(prefix_value_hbm.at[:, head], values_v.at[g, early]))
+        value_loads.append(load(suffix_value_hbm.at[:, head], values_v.at[g, late]))
+        key_loads.append(load(prefix_key_hbm.at[:, head], keys_v.at[g, early]))
+        key_loads.append(load(suffix_key_hbm.at[:, head], keys_v.at[g, late]))
+
+    barrier = pltpu.get_barrier_semaphore()
+    for a, b in peers:
+        pl.semaphore_signal(
+            barrier,
+            inc=1,
+            device_id={"pfx": other_p(a), "smp": other_s(b)},
+            device_id_type=pl.DeviceIdType.MESH,
+        )
+
+    hidden_load.wait()
+    hidden_wide = hidden_v[...].astype(jnp.float32)
+    normed_v[...] = (hidden_wide * gain_ref[...]).astype(jnp.bfloat16)
+    square_part = jnp.sum(hidden_wide * hidden_wide, axis=1, keepdims=True)
+    square_v[p] = jnp.broadcast_to(square_part, (rows, HEAD_WIDTH))
+    pl.semaphore_wait(barrier, len(peers))
+
+    sends = []
+    for step in steps:
+        copy = remote(square_v.at[p], square_v.at[p], square_sems, step, p, other_p(step), s)
+        copy.start()
+        sends.append(copy)
+
+    for slot, step in enumerate(order):
+        query_loads[slot].wait()
+        query_part[slot] = jnp.dot(
+            normed_v[...], query_weight_v[slot], preferred_element_type=jnp.float32
+        )
+        if step:
+            copy = remote(
+                query_part.at[slot], query_recv.at[p], query_sems, step, p, other_p(step), s
+            )
+            copy.start()
+            sends.append(copy)
+    for which in range(2):
+        new_loads[which].wait()
+        product = jnp.dot(
+            normed_v[...], new_weight_v[which], preferred_element_type=jnp.float32
+        )
+        for g in range(kv_heads):
+            new_part[g, :, which * HEAD_WIDTH : (which + 1) * HEAD_WIDTH] = product[
+                :, g * HEAD_WIDTH : (g + 1) * HEAD_WIDTH
+            ]
+    for step in steps:
+        copy = remote(
+            new_part.at[other_p(step) // pieces_per_kv],
+            new_recv.at[p],
+            new_sems,
+            step,
+            p,
+            other_p(step),
+            s,
+        )
+        copy.start()
+        sends.append(copy)
+
+    ones = jnp.ones((flipped_v.shape[1] - HEAD_WIDTH, key_count), jnp.bfloat16)
+
+    def eye(size):
+        return (
+            lax.broadcasted_iota(jnp.int32, (size, size), 0)
+            == lax.broadcasted_iota(jnp.int32, (size, size), 1)
+        ).astype(jnp.bfloat16)
+
+    by_last = (((1,), (1,)), ((), ()))
+    for copy in value_loads:
+        copy.wait()
+    for g in range(kv_heads):
+        flipped_v[g, :HEAD_WIDTH, :] = lax.dot_general(
+            eye(HEAD_WIDTH), values_v[g], by_last, preferred_element_type=jnp.float32
+        ).astype(jnp.bfloat16)
+        flipped_v[g, HEAD_WIDTH:, :] = ones
+    lane = lax.broadcasted_iota(jnp.int32, (suffix_len, lanes), 1)
+    position = lax.broadcasted_iota(jnp.int32, (suffix_len, lanes), 0) + p * suffix_len
+    lane_row = lax.rem(lane, rows)
+    lane_sample = jnp.full((suffix_len, lanes), -1, jnp.int32)
+    for row in range(rows):
+        lane_sample = jnp.where(lane_row == row, assign_ref[row] - s * rows, lane_sample)
+    own_lane = (lane >= s * piece_rows) & (lane < (s + 1) * piece_rows)
+    lane_sample = jnp.where(own_lane, lane_sample, -1)
+    for sample in range(rows):
+        live = (lane_sample == sample) & (position < lengths_ref[sample])
+        bias_v[sample * suffix_len : (sample + 1) * suffix_len, :] = jnp.where(
+            live, 0.0, very_negative
+        )
+
+    square_sum = square_v[p]
+    query_sum = query_part[len(steps)]
+    for step in steps:
+        source = other_p(step)
+        remote(square_v.at[p], square_v.at[source], square_sems, step, source, source, s).wait_recv()
+        remote(
+            query_part.at[0], query_recv.at[source], query_sems, step, source, source, s
+        ).wait_recv()
+        square_sum = square_sum + square_v[source]
+        query_sum = query_sum + query_recv[source]
+    rms_value = jnp.sqrt(square_sum / (width * pfx) + norm_eps)
+    own_rows = pl.ds(pl.multiple_of(s * piece_rows, piece_rows), piece_rows)
+    own_query = jnp.concatenate(
+        [
+            query_sum[:, h * HEAD_WIDTH : (h + 1) * HEAD_WIDTH] / rms_value
+            for h in range(piece_heads)
+        ],
+        axis=0,
+    ).astype(jnp.bfloat16)
+    queries_v[p, own_rows, :] = own_query
+    for a, b in peers:
+        copy = remote(
+            queries_v.at[p, own_rows],
+            queries_v.at[p, own_rows],
+            gather_sems,
+            a * smp + b,
+            me,
+            other_p(a),
+            other_s(b),
+        )
+        copy.start()
+        sends.append(copy)
+
+    for copy in key_loads:
+        copy.wait()
+    for a in [0] + steps:
+        to_p = other_p(a)
+        for b in range(smp):
+            if (a, b) != (0, 0):
+                to_s = other_s(b)
+                there = pl.ds(pl.multiple_of(to_s * piece_rows, piece_rows), piece_rows)
+                remote(
+                    queries_v.at[to_p, there],
+                    queries_v.at[to_p, there],
+                    gather_sems,
+                    a * smp + b,
+                    to_p * smp + to_s,
+                    to_p,
+                    to_s,
+                ).wait_recv()
+        g = to_p // pieces_per_kv
+        scores = lax.dot_general(
+            keys_v[g], queries_v[to_p], by_last, preferred_element_type=jnp.float32
+        )
+        prefix_scores = scores[:prefix_count]
+        suffix_scores = scores[prefix_count:] + bias_v[...]
+        top = jnp.maximum(
+            jnp.max(prefix_scores, axis=0, keepdims=True),
+            jnp.max(suffix_scores, axis=0, keepdims=True),
+        )
+        weights = jnp.concatenate(
+            [
+                jnp.exp2((prefix_scores - top) * power_scale).astype(jnp.bfloat16),
+                jnp.exp2((suffix_scores - top) * power_scale).astype(jnp.bfloat16),
+            ],
+            axis=0,
+        )
+        sums = jnp.dot(flipped_v[g], weights, preferred_element_type=jnp.float32)
+        numer_send[to_p] = lax.dot_general(
+            eye(lanes),
+            sums[:HEAD_WIDTH].astype(jnp.bfloat16),
+            by_last,
+            preferred_element_type=jnp.float32,
+        ).astype(jnp.bfloat16)
+        stat_row = lax.broadcasted_iota(jnp.int32, (8, lanes), 0)
+        stat_send[to_p] = jnp.where(
+            stat_row == 0, top, sums[HEAD_WIDTH : HEAD_WIDTH + 8]
+        )
+        for b in range(smp):
+            to_s = other_s(b)
+            there = pl.ds(pl.multiple_of(to_s * piece_rows, piece_rows), piece_rows)
+            if (a, b) == (0, 0):
+                numer_recv[me] = numer_send[to_p, there, :]
+                stat_recv[me] = stat_send[to_p]
+            else:
+                index = a * smp + b
+                for copy in (
+                    remote(
+                        numer_send.at[to_p, there], numer_recv.at[me], numer_sems, index, me, to_p, to_s
+                    ),
+                    remote(stat_send.at[to_p], stat_recv.at[me], stat_sems, index, me, to_p, to_s),
+                ):
+                    copy.start()
+                    sends.append(copy)
+
+    new_sum = new_part[p // pieces_per_kv]
+    for step in steps:
+        source = other_p(step)
+        remote(new_part.at[0], new_recv.at[source], new_sems, step, source, source, s).wait_recv()
+        new_sum = new_sum + new_recv[source]
+    new_key = (new_sum[:, :HEAD_WIDTH] / rms_value).astype(jnp.bfloat16).astype(jnp.float32)
+    new_value = (new_sum[:, HEAD_WIDTH:] / rms_value).astype(jnp.bfloat16).astype(jnp.float32)
+    own_score = jnp.sum(
+        own_query.astype(jnp.float32) * jnp.concatenate([new_key] * piece_heads, axis=0),
+        axis=1,
+        keepdims=True,
+    )
+    own_value = jnp.concatenate([new_value] * piece_heads, axis=0)
+    for a, b in peers:
+        from_p, from_s = other_p(a), other_s(b)
+        source = from_p * smp + from_s
+        remote(
+            numer_send.at[p, own_rows], numer_recv.at[source], numer_sems, a * smp + b, source, from_p, from_s
+        ).wait_recv()
+        remote(
+            stat_send.at[p], stat_recv.at[source], stat_sems, a * smp + b, source, from_p, from_s
+        ).wait_recv()
+    stats = [stat_recv[i] for i in range(sources)]
+    spare = lanes - 8 * sources
+    if spare:
+        stats.append(jnp.zeros((spare, lanes), jnp.float32))
+    column_v[...] = jnp.concatenate(stats, axis=0).T
+    columns = column_v[own_rows, :]
+    top = own_score
+    for i in range(sources):
+        top = jnp.maximum(top, columns[:, 8 * i : 8 * i + 1])
+    own_weight = jnp.exp2((own_score - top) * power_scale).astype(jnp.bfloat16).astype(jnp.float32)
+    factors = jnp.exp2(jnp.minimum(columns - top, 0.0) * power_scale)
+    numerator = own_weight * own_value
+    denominator = own_weight
+    for i in range(sources):
+        factor = factors[:, 8 * i : 8 * i + 1]
+        numerator = numerator + factor * numer_recv[i].astype(jnp.float32)
+        denominator = denominator + factor * columns[:, 8 * i + 1 : 8 * i + 2]
+    out_v[p] = (numerator / denominator).astype(jnp.bfloat16)
+    for step in steps:
+        copy = remote(out_v.at[p], out_v.at[p], out_sems, step, p, other_p(step), s)
+        copy.start()
+        sends.append(copy)
+    for step in steps:
+        source = other_p(step)
+        remote(out_v.at[p], out_v.at[source], out_sems, step, source, source, s).wait_recv()
+    for piece in range(pfx):
+        for h in range(piece_heads):
+            start = (piece * piece_heads + h) * HEAD_WIDTH
+            out_ref[:, start : start + HEAD_WIDTH] = out_v[piece, h * rows : (h + 1) * rows, :]
+    for copy in sends:
+        copy.wait_send()
+
+
+def kernel_body(
+    pfx,
+    smp,
+    hidden,
+    norm_gain,
+    query_weight,
+    key_matrix,
+    value_matrix,
+    prefix_key,
+    shared_prefix_value,
+    sample_suffix_key,
+    sample_suffix_value,
+    lengths,
+    assign,
+):
+    rows, width = hidden.shape
+    query_cols = query_weight.shape[1]
+    kv_cols = key_matrix.shape[1]
+    kv_heads = kv_cols // HEAD_WIDTH
+    piece_cols = query_cols // pfx
+    piece_rows = piece_cols // HEAD_WIDTH * rows
+    lanes = smp * piece_rows
+    sources = pfx * smp
+    suffix_count = rows * sample_suffix_key.shape[1]
+    key_count = prefix_key.shape[0] + suffix_count
+    wide, narrow = jnp.float32, jnp.bfloat16
+    anywhere = pl.BlockSpec(memory_space=pl.ANY)
+    scratch = [
+        pltpu.VMEM((rows, width), narrow),
+        pltpu.VMEM((rows, width), narrow),
+        pltpu.VMEM((pfx, width, piece_cols), narrow),
+        pltpu.VMEM((2, width, kv_cols), narrow),
+        pltpu.VMEM((kv_heads, key_count, HEAD_WIDTH), narrow),
+        pltpu.VMEM((kv_heads, key_count, HEAD_WIDTH), narrow),
+        pltpu.VMEM((kv_heads, HEAD_WIDTH + 16, key_count), narrow),
+        pltpu.VMEM((suffix_count, lanes), wide),
+        pltpu.VMEM((pfx, rows, HEAD_WIDTH), wide),
+        pltpu.VMEM((pfx, rows, piece_cols), wide),
+        pltpu.VMEM((pfx, rows, piece_cols), wide),
+        pltpu.VMEM((kv_heads, rows, 2 * HEAD_WIDTH), wide),
+        pltpu.VMEM((pfx, rows, 2 * HEAD_WIDTH), wide),
+        pltpu.VMEM((pfx, lanes, HEAD_WIDTH), narrow),
+        pltpu.VMEM((pfx, lanes, HEAD_WIDTH), narrow),
+        pltpu.VMEM((pfx, 8, lanes), wide),
+        pltpu.VMEM((sources, piece_rows, HEAD_WIDTH), narrow),
+        pltpu.VMEM((sources, 8, lanes), wide),
+        pltpu.VMEM((lanes, lanes), wide),
+        pltpu.VMEM((pfx, piece_rows, HEAD_WIDTH), narrow),
+        pltpu.SemaphoreType.DMA((3 + pfx + 4 * kv_heads,)),
+        pltpu.SemaphoreType.DMA((2, pfx)),
+        pltpu.SemaphoreType.DMA((2, pfx)),
+        pltpu.SemaphoreType.DMA((2, pfx)),
+        pltpu.SemaphoreType.DMA((2, sources)),
+        pltpu.SemaphoreType.DMA((2, sources)),
+        pltpu.SemaphoreType.DMA((2, sources)),
+        pltpu.SemaphoreType.DMA((2, pfx)),
+    ]
+    return pl.pallas_call(
+        functools.partial(group_kernel, pfx, smp),
+        out_shape=jax.ShapeDtypeStruct((rows, query_cols), narrow),
+        in_specs=[anywhere, pl.BlockSpec(memory_space=pltpu.VMEM)]
+        + [anywhere] * 7
+        + [pl.BlockSpec(memory_space=pltpu.SMEM)] * 2,
+        out_specs=pl.BlockSpec(memory_space=pltpu.VMEM),
+        scratch_shapes=scratch,
+        compiler_params=pltpu.CompilerParams(
+            collective_id=0, has_side_effects=True, vmem_limit_bytes=40 * 1024 * 1024
+        ),
+    )(
+        hidden,
+        norm_gain.astype(wide).reshape(1, -1),
+        query_weight,
+        key_matrix,
+        value_matrix,
+        prefix_key,
+        shared_prefix_value,
+        sample_suffix_key.reshape(suffix_count, kv_cols),
+        sample_suffix_value.reshape(suffix_count, kv_cols),
+        lengths,
+        assign,
+    )
+
+
+def body(hidden, norm_gain, query_weight, key_matrix, *rest, pfx, smp):
+    rows = hidden.shape[0]
+    local_heads = query_weight.shape[1] // HEAD_WIDTH
+    local_kv = key_matrix.shape[1] // HEAD_WIDTH
+    lanes = smp * (local_heads // pfx) * rows
+    if local_heads % pfx == 0 and pfx % local_kv == 0 and lanes == 128 and pfx * smp <= 16:
+        chosen = functools.partial(kernel_body, pfx, smp)
+    else:
+        chosen = plain_body
+    return chosen(hidden, norm_gain, query_weight, key_matrix, *rest)
+
+
 def solution(mesh):
     return jax.shard_map(
-        body,
+        functools.partial(body, pfx=mesh.shape["pfx"], smp=mesh.shape["smp"]),
         mesh=mesh,
         in_specs=(
             P(("groups", "smp"), "pfx"),

time: 151 us -> 43.9 us (0.29)
  blocking collectives: 58.3 us -> 0 us
  waiting for transfers between devices: 54.3 us -> 0 us
  Pallas kernels: 0 us -> 30.1 us
  between operations: 13.4 us -> 0.02 us
  matrix products: 11.2 us -> 0 us
  other arithmetic: 7.82 us -> 0.69 us
  local copies, waits for them, and re-layouts: 5.68 us -> 12.6 us
    psum x2 -> x0, waiting for transfers between devices: 49 us -> none  [the longest x1 36 us: body(): lax.psum(block_numer.astype(jnp.bfloat16), 'pfx').astype(jnp.float32)]
    psum x2 -> x0, blocking collectives: 33 us -> none  [the longest x1 21.3 us: body(): lax.psum((query_part, key_part, value_part, square_part), 'pfx')]
    pallas_call x0 -> x1, Pallas kernels: none -> 30.1 us  [kernel_body(): pl.pallas_call(functools.partial(group_kernel, pfx, smp), out_shape=jax.S...]
    pmax x1 -> x0, blocking collectives: 20.4 us -> none  [body(): global_top = lax.pmax(local_top, ('pfx', 'smp'))]
    dot_general x13 -> x0, matrix products: 11.2 us -> none  [the longest x1 5.42 us: body(): jnp.dot(normed, query_weight, preferred_element_type=jnp.float32)]
    unnamed x22 -> x21, local copies, waits for them, and re-layouts: 2.58 us -> 12.6 us
    unnamed x5 -> x0, waiting for transfers between devices: 5.1 us -> none
    all_gather x1 -> x0, blocking collectives: 4.94 us -> none  [body(): all_queries = lax.all_gather(query_rows, 'smp', axis=0, tiled=True)]
  transfers between devices with their start and end apart: 4 -> 0, of which waited for: 4 -> 0; matrix products, arithmetic and copies ran while one was open for 4% -> 0% of each run, Pallas kernels for 0% -> 0%
where the time goes in v1:
time: 43.9 us; the launch traced here: 43.4 us
  Pallas kernels  30.1 us (69%)
  local copies, waits for them, and re-layouts  12.6 us (29%)
  other arithmetic  0.69 us (2%)
    pallas_call x1, Pallas kernels, kernel_body(): pl.pallas_call(functools.partial(group_kernel, pfx, smp), out_shape=jax.S...  30.1 us
    unnamed x21, local copies, waits for them, and re-layouts  12.6 us

profile of v1, /device:TPU:0, one launch (start us, length us, event | category | flops | bytes accessed | tf_op | source)
XLA Modules:
  0.0 43.4 jit_solution(13072804877148172865)
XLA Ops:
  0.0 0.7 %reshape.15 = f32[2048]{0:T(1024)S(1)} convert(bf16[2048]{0:T(1024)(128)(2,1)} %param.12) | non-fusion elementwise | flops 2048 | bytes 12288 | tf_op jit(solution)/shard_map/reshape | solution.py:584
  0.7 0.0 copy-start
  0.7 3.4 %copy-done = bf16[2048,2048]{1,0:T(8,128)(2,1)S(1)} copy-done((bf16[2048,2048]{1,0:T(8,128)(2,1)S(1)}, bf16[2048,2048]{1,0:T(8,128)(2,1)}, u32[]{:S(2)}) %copy-start) | copy-done | bytes 8388632
  4.1 0.0 copy-start.1
  4.1 1.2 %copy-done.1 = bf16[2048,256]{1,0:T(8,128)(2,1)S(1)} copy-done((bf16[2048,256]{1,0:T(8,128)(2,1)S(1)}, bf16[2048,256]{1,0:T(8,128)(2,1)}, u32[]{:S(2)}) %copy-start.1) | copy-done | bytes 1048600
  5.3 0.0 copy-start.2
  5.3 1.2 %copy-done.2 = bf16[2048,256]{1,0:T(8,128)(2,1)S(1)} copy-done((bf16[2048,256]{1,0:T(8,128)(2,1)S(1)}, bf16[2048,256]{1,0:T(8,128)(2,1)}, u32[]{:S(2)}) %copy-start.2) | copy-done | bytes 1048600
  6.5 0.0 copy-start.3
  6.5 1.0 %copy-done.3 = bf16[1024,256]{1,0:T(8,128)(2,1)S(1)} copy-done((bf16[1024,256]{1,0:T(8,128)(2,1)S(1)}, bf16[1024,256]{1,0:T(8,128)(2,1)}, u32[]{:S(2)}) %copy-start.3) | copy-done | bytes 524312
  7.6 0.0 copy-start.4
  7.6 1.0 %copy-done.4 = bf16[1024,256]{1,0:T(8,128)(2,1)S(1)} copy-done((bf16[1024,256]{1,0:T(8,128)(2,1)S(1)}, bf16[1024,256]{1,0:T(8,128)(2,1)}, u32[]{:S(2)}) %copy-start.4) | copy-done | bytes 524312
  8.6 0.0 copy-start.5
  8.6 0.9 %copy-done.5 = bf16[16,32,256]{2,1,0:T(8,128)(2,1)S(1)} copy-done((bf16[16,32,256]{2,1,0:T(8,128)(2,1)S(1)}, bf16[16,32,256]{2,1,0:T(8,128)(2,1)}, u32[]{:S(2)}) %copy-start.5) | copy-done | bytes 262168
  9.6 0.0 copy-start.6
  9.6 0.9 %copy-done.6 = bf16[16,32,256]{2,1,0:T(8,128)(2,1)S(1)} copy-done((bf16[16,32,256]{2,1,0:T(8,128)(2,1)S(1)}, bf16[16,32,256]{2,1,0:T(8,128)(2,1)}, u32[]{:S(2)}) %copy-start.6) | copy-done | bytes 262168
  10.5 0.0 copy-start.7
  10.5 0.8 %copy-done.7 = bf16[16,2048]{1,0:T(8,128)(2,1)S(1)} copy-done((bf16[16,2048]{1,0:T(8,128)(2,1)S(1)}, bf16[16,2048]{1,0:T(8,128)(2,1)}, u32[]{:S(2)}) %copy-start.7) | copy-done | bytes 65560
  11.3 0.0 copy-start.8
  11.3 0.7 %copy-done.8 = s32[16]{0:T(128)S(1)} copy-done((s32[16]{0:T(128)S(1)}, s32[16]{0:T(128)}, u32[]{:S(2)}) %copy-start.8) | copy-done | bytes 88
  12.0 0.0 copy-start.9
  12.0 0.7 %copy-done.9 = s32[16]{0:T(128)S(1)} copy-done((s32[16]{0:T(128)S(1)}, s32[16]{0:T(128)}, u32[]{:S(2)}) %copy-start.9) | copy-done | bytes 88
  12.7 30.1 %shard_map.109 = bf16[16,2048]{1,0:T(8,128)(2,1)S(1)} custom-call(bf16[16,2048]{1,0:T(8,128)(2,1)S(1)} %copy-done.7, f32[1,2048]{1,0:T(1,128)S(1)} %bitcast.5, bf16[2048,2048]{1,0:T(8,128)(2,1)S(1)} %copy-done, bf16[2048,256]{1,0:T(8,128)(2,1)S(1)} %copy-done.1, bf16[2048,256]{1,0:T(8,128)(2,1)S(1)} %copy-done.2, bf16[1024,256]{1,0:T(8,128)(2,1)S(1)} %copy-done.3, ...), custom_call_target="tpu_custom_call" | custom-call | tf_op jit(solution)/shard_map/pallas_call | solution.py:571
  42.8 0.6 %copy.13 = bf16[16,2048]{1,0:T(8,128)(2,1)} copy(bf16[16,2048]{1,0:T(8,128)(2,1)S(1)} %shard_map.109) | data formatting | bytes 131072
Async XLA Ops:
  0.7 3.4 %copy-start = (bf16[2048,2048]{1,0:T(8,128)(2,1)S(1)}, bf16[2048,2048]{1,0:T(8,128)(2,1)}, u32[]{:S(2)}) copy-start(bf16[2048,2048]{1,0:T(8,128)(2,1)} %query_weight_hbm.1) | copy-start | bytes 25165828
  4.1 1.2 %copy-start.1 = (bf16[2048,256]{1,0:T(8,128)(2,1)S(1)}, bf16[2048,256]{1,0:T(8,128)(2,1)}, u32[]{:S(2)}) copy-start(bf16[2048,256]{1,0:T(8,128)(2,1)} %key_matrix_hbm.1) | copy-start | bytes 3145732
  5.3 1.2 %copy-start.2 = (bf16[2048,256]{1,0:T(8,128)(2,1)S(1)}, bf16[2048,256]{1,0:T(8,128)(2,1)}, u32[]{:S(2)}) copy-start(bf16[2048,256]{1,0:T(8,128)(2,1)} %value_matrix_hbm.1) | copy-start | bytes 3145732
  6.5 1.0 %copy-start.3 = (bf16[1024,256]{1,0:T(8,128)(2,1)S(1)}, bf16[1024,256]{1,0:T(8,128)(2,1)}, u32[]{:S(2)}) copy-start(bf16[1024,256]{1,0:T(8,128)(2,1)} %prefix_key_hbm.1) | copy-start | bytes 1572868
  7.6 1.0 %copy-start.4 = (bf16[1024,256]{1,0:T(8,128)(2,1)S(1)}, bf16[1024,256]{1,0:T(8,128)(2,1)}, u32[]{:S(2)}) copy-start(bf16[1024,256]{1,0:T(8,128)(2,1)} %prefix_value_hbm.1) | copy-start | bytes 1572868
  8.6 0.9 %copy-start.5 = (bf16[16,32,256]{2,1,0:T(8,128)(2,1)S(1)}, bf16[16,32,256]{2,1,0:T(8,128)(2,1)}, u32[]{:S(2)}) copy-start(bf16[16,32,256]{2,1,0:T(8,128)(2,1)} %param.18) | copy-start | bytes 786436
  9.6 0.9 %copy-start.6 = (bf16[16,32,256]{2,1,0:T(8,128)(2,1)S(1)}, bf16[16,32,256]{2,1,0:T(8,128)(2,1)}, u32[]{:S(2)}) copy-start(bf16[16,32,256]{2,1,0:T(8,128)(2,1)} %param.19) | copy-start | bytes 786436
  10.5 0.8 %copy-start.7 = (bf16[16,2048]{1,0:T(8,128)(2,1)S(1)}, bf16[16,2048]{1,0:T(8,128)(2,1)}, u32[]{:S(2)}) copy-start(bf16[16,2048]{1,0:T(8,128)(2,1)} %hidden_hbm.1) | copy-start | bytes 196612
  11.3 0.7 %copy-start.8 = (s32[16]{0:T(128)S(1)}, s32[16]{0:T(128)}, u32[]{:S(2)}) copy-start(s32[16]{0:T(128)} %lengths_ref.1) | copy-start | bytes 196
  12.0 0.7 %copy-start.9 = (s32[16]{0:T(128)S(1)}, s32[16]{0:T(128)}, u32[]{:S(2)}) copy-start(s32[16]{0:T(128)} %assign_ref.1) | copy-start | bytes 196

commit v2 on v1

--- a/solution.py
+++ b/solution.py
@@ -229,13 +229,18 @@
     me = p * smp + s
 
     def other_p(step):
-        return lax.rem(p + step, pfx)
+        partner, bit = p, 1
+        while bit < pfx:
+            if step & bit:
+                partner = partner + bit - 2 * bit * lax.rem(p // bit, 2)
+            bit *= 2
+        return partner
 
     def other_s(step):
         return lax.rem(s + step, smp)
 
-    steps = sorted(range(1, pfx), key=lambda step: -min(step, pfx - step))
-    order = steps + [0]
+    steps = list(range(1, pfx))
+    order = [step for step in steps if step > 1] + [1, 0]
     peers = [(a, b) for a in [0] + steps for b in range(smp) if (a, b) != (0, 0)]
 
     def remote(source, target, sems, send_index, recv_index, to_p, to_s):
@@ -287,7 +292,7 @@
 
     hidden_load.wait()
     hidden_wide = hidden_v[...].astype(jnp.float32)
-    normed_v[...] = (hidden_wide * gain_ref[...]).astype(jnp.bfloat16)
+    normed_v[...] = (hidden_wide * gain_ref[...].astype(jnp.float32).reshape(1, width)).astype(jnp.bfloat16)
     square_part = jnp.sum(hidden_wide * hidden_wide, axis=1, keepdims=True)
     square_v[p] = jnp.broadcast_to(square_part, (rows, HEAD_WIDTH))
     pl.semaphore_wait(barrier, len(peers))
@@ -362,7 +367,7 @@
         )
 
     square_sum = square_v[p]
-    query_sum = query_part[len(steps)]
+    query_sum = query_part[order.index(0)]
     for step in steps:
         source = other_p(step)
         remote(square_v.at[p], square_v.at[source], square_sems, step, source, source, s).wait_recv()
@@ -537,7 +542,7 @@
     suffix_count = rows * sample_suffix_key.shape[1]
     key_count = prefix_key.shape[0] + suffix_count
     wide, narrow = jnp.float32, jnp.bfloat16
-    anywhere = pl.BlockSpec(memory_space=pl.ANY)
+    anywhere = pl.BlockSpec(memory_space=pltpu.HBM)
     scratch = [
         pltpu.VMEM((rows, width), narrow),
         pltpu.VMEM((rows, width), narrow),
@@ -577,11 +582,11 @@
         out_specs=pl.BlockSpec(memory_space=pltpu.VMEM),
         scratch_shapes=scratch,
         compiler_params=pltpu.CompilerParams(
-            collective_id=0, has_side_effects=True, vmem_limit_bytes=40 * 1024 * 1024
+            collective_id=0, has_side_effects=True, vmem_limit_bytes=56 * 1024 * 1024
         ),
     )(
         hidden,
-        norm_gain.astype(wide).reshape(1, -1),
+        norm_gain,
         query_weight,
         key_matrix,
         value_matrix,
@@ -599,7 +604,8 @@
     local_heads = query_weight.shape[1] // HEAD_WIDTH
     local_kv = key_matrix.shape[1] // HEAD_WIDTH
     lanes = smp * (local_heads // pfx) * rows
-    if local_heads % pfx == 0 and pfx % local_kv == 0 and lanes == 128 and pfx * smp <= 16:
+    whole = local_heads % pfx == 0 and pfx % local_kv == 0 and pfx & (pfx - 1) == 0
+    if whole and lanes == 128 and 8 * pfx * smp <= lanes:
         chosen = functools.partial(kernel_body, pfx, smp)
     else:
         chosen = plain_body

time: 43.9 us -> 30.1 us (0.69)
  local copies, waits for them, and re-layouts: 12.6 us -> 1.47 us
  Pallas kernels: 30.1 us -> 28.5 us
  other arithmetic: 0.69 us -> 0 us
    unnamed x21 -> x1, local copies, waits for them, and re-layouts: 12.6 us -> 1.47 us
    pallas_call x1, Pallas kernels: 30.1 us -> 28.5 us  [kernel_body(): pl.pallas_call(functools.partial(group_kernel, pfx, smp), out_shape=jax.S...]
    reshape x1 -> x0, other arithmetic: 0.69 us -> none  [kernel_body(): norm_gain.astype(wide).reshape(1, -1)]
where the time goes in v2:
time: 30.1 us; the launch traced here: 29.9 us
  Pallas kernels  28.5 us (95%)
  local copies, waits for them, and re-layouts  1.47 us (5%)
    pallas_call x1, Pallas kernels, kernel_body(): pl.pallas_call(functools.partial(group_kernel, pfx, smp), out_shape=jax.S...  28.5 us
    unnamed x1, local copies, waits for them, and re-layouts  1.47 us

profile of v2, /device:TPU:0, one launch (start us, length us, event | category | flops | bytes accessed | tf_op | source)
XLA Modules:
  0.0 29.9 jit_solution(4097575489091591839)
XLA Ops:
  0.0 28.5 %shard_map.109 = bf16[16,2048]{1,0:T(8,128)(2,1)} custom-call(bf16[16,2048]{1,0:T(8,128)(2,1)} %hidden_hbm.1, bf16[2048]{0:T(1024)(128)(2,1)} %gain_ref.1, bf16[2048,2048]{1,0:T(8,128)(2,1)} %query_weight_hbm.1, bf16[2048,256]{1,0:T(8,128)(2,1)} %key_matrix_hbm.1, bf16[2048,256]{1,0:T(8,128)(2,1)} %value_matrix_hbm.1, bf16[1024,256]{1,0:T(8,128)(2,1)} %prefix_key_hbm.1, ...), custom_call_target="tpu_custom_call" | custom-call | tf_op jit(solution)/shard_map/pallas_call | solution.py:576
  28.5 1.5 %copy.13 = bf16[16,2048]{1,0:T(8,128)(2,1)} copy(bf16[16,2048]{1,0:T(8,128)(2,1)} %shard_map.109) | data formatting | bytes 131072
